TPU v7x, 32 devices: a whole 2x2x4 slice. The times are simulated.
32 devices in a mesh: grp: 2 (over y), ctx: 16 (over z, x, core).
Axes of the slice: x: 2, y: 2, z: 4, core: 2. Of those that a mesh axis runs over, the one named last changes fastest.
Arguments:
- queries: bfloat16 [4096, 4096], P(('grp', 'ctx')), parts along dimension 0, may hold values from -6 to 6
- key_matrix: bfloat16 [4096, 512], P(('grp', 'ctx')), parts along dimension 0, may hold values from -6 to 6
- value_matrix: bfloat16 [4096, 512], P(('grp', 'ctx')), parts along dimension 0, may hold values from -6 to 6
- outputs: bfloat16 [4096, 4096], P(('grp', 'ctx')), parts along dimension 0, may hold values from -6 to 6
- output_gradient: bfloat16 [4096, 4096], P(('grp', 'ctx')), parts along dimension 0, may hold values from -6 to 6
- log_normalizer: float32 [32, 4096], P(None, ('grp', 'ctx')), parts along dimension 1, may hold values from 2 to 6
- doc_lengths: int32 [16], P('grp'), parts along dimension 0, may hold values from 1 to 512, 2048 in all
Outputs:
- query_grad: bfloat16 [4096, 4096], P(('grp', 'ctx')), parts along dimension 0
- key_grad: bfloat16 [4096, 512], P(('grp', 'ctx')), parts along dimension 0
- value_grad: bfloat16 [4096, 512], P(('grp', 'ctx')), parts along dimension 0
There are 2 independent parts, one for each index of `grp`. A program takes and returns all parts, laid end to end along the dimension named above; each array names one. Nothing has to cross between parts.
Inputs may be any that keep to these rules, and one draw needn't show every extreme that they name: `doc_lengths`: the lengths sum to 2048; the longest document has exactly 512 tokens.
All inputs are finite; a program needn't handle non-finite values.
Results may differ from a plain program's by a relative error of at most 0.0066.
Values may be sent and summed in bfloat16 or wider, within the bound.
A program may use at most 64 MiB of HBM per device.

v0:
```python
import math

import jax
import jax.numpy as jnp
from jax import lax
from jax.sharding import PartitionSpec as P

KEY_VALUE_HEADS = 4
HEAD_SIZE = 128
QUERY_HEADS = 32
SPAN = 4


def shifted(block, axis, distance):
    devices = range(lax.axis_size(axis))
    route = [(i - distance, i) for i in devices if i - distance in devices]
    return lax.ppermute(block, axis, route)


def doc_index(doc_lengths, positions):
    doc_ends = jnp.cumsum(doc_lengths)
    return jnp.sum((positions[:, None] >= doc_ends[None, :]).astype(jnp.int32), axis=1)


def body(queries, key_matrix, value_matrix, outputs, output_gradient, log_normalizer, doc_lengths):
    token_count = queries.shape[0]
    head_group = QUERY_HEADS // KEY_VALUE_HEADS
    key_value_columns = KEY_VALUE_HEADS * HEAD_SIZE
    inv_root = 1.0 / math.sqrt(HEAD_SIZE)
    my_index = lax.axis_index("ctx")
    my_start = my_index * token_count
    local_rows = jnp.arange(token_count, dtype=jnp.int32)
    query_pos = my_start + local_rows
    query_doc = doc_index(doc_lengths, query_pos)
    query_per_head = queries.reshape(token_count, KEY_VALUE_HEADS, head_group, HEAD_SIZE)
    gradient_per_head = output_gradient.reshape(token_count, KEY_VALUE_HEADS, head_group, HEAD_SIZE)
    output_per_head = outputs.reshape(token_count, KEY_VALUE_HEADS, head_group, HEAD_SIZE)
    row_dot = jnp.transpose(
        jnp.sum(
            gradient_per_head.astype(jnp.float32) * output_per_head.astype(jnp.float32), axis=3
        ),
        (1, 2, 0),
    )
    normalizer_per_head = log_normalizer.reshape(KEY_VALUE_HEADS, head_group, token_count, 1)

    def attend(key_value_pair, offset):
        key_tile = key_value_pair[0].reshape(token_count, KEY_VALUE_HEADS, HEAD_SIZE)
        value_tile = key_value_pair[1].reshape(token_count, KEY_VALUE_HEADS, HEAD_SIZE)
        key_pos = my_start - offset * token_count + local_rows
        key_doc = doc_index(doc_lengths, key_pos)
        allowed = (key_pos[None, :] <= query_pos[:, None]) & (key_pos[None, :] >= 0)
        allowed = allowed & (query_doc[:, None] == key_doc[None, :])
        scores = (
            jnp.einsum(
                "tkgd,skd->kgts", query_per_head, key_tile, preferred_element_type=jnp.float32
            )
            * inv_root
        )
        weights = jnp.where(allowed, jnp.exp(scores - normalizer_per_head), 0.0)
        weights_low = weights.astype(jnp.bfloat16)
        grad_prob = jnp.einsum(
            "tkgd,skd->kgts", gradient_per_head, value_tile, preferred_element_type=jnp.float32
        )
        grad_score = (weights * (grad_prob - row_dot[..., None]) * inv_root).astype(jnp.bfloat16)
        query_part = jnp.einsum(
            "kgts,skd->tkgd", grad_score, key_tile, preferred_element_type=jnp.float32
        )
        key_part = jnp.einsum(
            "kgts,tkgd->skd", grad_score, query_per_head, preferred_element_type=jnp.float32
        ).reshape(token_count, key_value_columns)
        value_part = jnp.einsum(
            "kgts,tkgd->skd", weights_low, gradient_per_head, preferred_element_type=jnp.float32
        ).reshape(token_count, key_value_columns)
        return (query_part, jnp.stack([key_part, value_part]))

    key_value_pair = jnp.stack([key_matrix, value_matrix])
    query_total, key_total = attend(key_value_pair, 0)
    partials = []
    arrived = key_value_pair
    for offset in range(1, SPAN + 1):
        arrived = shifted(arrived, "ctx", 1)
        query_part, kv_part = attend(arrived, offset)
        query_total = query_total + query_part
        partials.append(kv_part)
    returned = jnp.zeros((2, token_count, key_value_columns), jnp.float32)
    for offset in range(SPAN, 0, -1):
        returned = shifted(returned + partials[offset - 1], "ctx", -1)
    key_total = key_total + returned
    query_grad = query_total.reshape(token_count, QUERY_HEADS * HEAD_SIZE).astype(jnp.bfloat16)
    return (query_grad, key_total[0].astype(jnp.bfloat16), key_total[1].astype(jnp.bfloat16))


def solution(mesh):
    in_specs = (
        P(("grp", "ctx"), None),
        P(("grp", "ctx"), None),
        P(("grp", "ctx"), None),
        P(("grp", "ctx"), None),
        P(("grp", "ctx"), None),
        P(None, ("grp", "ctx")),
        P("grp"),
    )
    out_specs = (P(("grp", "ctx"), None), P(("grp", "ctx"), None), P(("grp", "ctx"), None))
    return jax.shard_map(body, mesh=mesh, in_specs=in_specs, out_specs=out_specs, check_vma=False)
```

profile of v0, /device:TPU:19, one launch (start us, length us, event | category | flops | bytes accessed | tf_op | source)
XLA Modules:
  0.0 123.2 jit_solution(454553143958668566)
XLA Ops:
  0.6 1.1 copy.189
  1.8 1.0 copy.190
  3.5 3.7 %collective-permute-start = (bf16[2,128,512]{1,2,0:T(8,128)(2,1)}, bf16[2,128,512]{1,2,0:T(8,128)(2,1)}, u32[]{:S(2)}, u32[]{:S(2)}) collective-permute-start(bf16[2,128,512]{1,2,0:T(8,128)(2,1)} %pad_maximum_fusion.1), channel_id=1, source_target_pairs={{0,1},{1,2},{2,3},{3,4},{4,5},{5,6},{6,7},{7,8},{8,9},{9,10},{10,1... | collective-permute-start | bytes 786440 | tf_op jit(solution)/shard_map/ppermute | solution.py:17
  10.8 1.6 %reshape_squeeze_stack.6 = bf16[128,4,128]{2,1,0:T(4,128)(2,1)} reshape(bf16[128,512]{1,0:T(8,128)(2,1)} %param.8) | data formatting | bytes 262144 | tf_op jit(solution)/shard_map/reshape;squeeze;stack | solution.py:47
  14.0 1.4 %copy.305 = bf16[16,8,32,128]{3,2,1,0:T(8,128)(2,1)S(1)} copy(bf16[16,8,32,128]{3,1,2,0:T(8,128)(2,1)} %bitcast.293) | data formatting | bytes 2097152
  15.4 1.0 copy.214
  16.4 1.4 %convert_bitcast_fusion = f32[16,8,32,128]{3,1,2,0:T(8,128)S(1)} fusion(bf16[128,4096]{1,0:T(8,128)(2,1)} %param.10), kind=kLoop, calls=%fused_computation.40 | loop fusion | flops 524288 | bytes 3145728
  19.2 1.1 copy.245
  21.9 1.7 %compare_and_fusion = (pred[128,128]{0,1:T(8,128)(4,1)}, pred[128,128]{0,1:T(8,128)(4,1)}, pred[128,128]{0,1:T(8,128)(4,1)}, pred[128,128]{0,1:T(8,128)(4,1)}, pred[128,128]{0,1:T(8,128)(4,1)S(1)}) fusion(s32[128]{0:T(128)S(1)} %get-tuple-element.19, s32[128]{0:T(128)} %iota_add_fusion.4, s32[128]{0:T(128)S(1)} %get-tuple-element.15, ...), kind=kLoop, calls=%fused_computation.62 | loop fusion | flops 327680 | bytes 87680 | tf_op jit(solution)/shard_map/and | solution.py:52
  23.5 1.3 %fusion.25 = f32[4,8,128,128]{2,3,1,0:T(8,128)S(1)} fusion(bf16[128,4,128,1]{0,2,3,1:T(8,128)(2,1)S(1)} %copy.245, bf16[128,4,8,128]{0,3,2,1:T(8,128)(2,1)S(1)} %bitcast.266, f32[4,8,128]{2,1,0:T(8,128)} %bitcast.308, pred[128,128]{0,1:T(8,128)(4,1)S(1)} %get-tuple-element.34), kind=kOutput, calls=%fused_computation.39 | convolution fusion | flops 135790592 | bytes 3309568 | tf_op jit(solution)/shard_map/tkgd,skd->kgts/dot_general | solution.py:54
  24.9 1.2 fusion.34
  27.8 1.8 %copy.216 = f32[1,128,512]{2,1,0:T(8,128)} copy(f32[1,128,512]{1,2,0:T(8,128)} %bitcast.295) | data formatting | bytes 524288 | tf_op jit(solution)/shard_map/stack;reshape | solution.py:74
  29.6 1.8 %fusion.50 = f32[4,8,128,128]{2,3,1,0:T(8,128)} fusion(bf16[128,4,128,1]{0,2,3,1:T(8,128)(2,1)S(1)} %copy.245, bf16[4,8,128,128]{2,3,1,0:T(8,128)(2,1)S(1)} %fusion.23), kind=kOutput, calls=%fused_computation.94 | convolution fusion | flops 134217728 | bytes 3276800 | tf_op jit(solution)/shard_map/kgts,skd->tkgd/dot_general | solution.py:65
  31.4 1.0 fusion.39
  35.6 1.9 %collective-permute-start.1 = (bf16[2,128,512]{1,2,0:T(8,128)(2,1)}, bf16[2,128,512]{1,2,0:T(8,128)(2,1)}, u32[]{:S(2)}, u32[]{:S(2)}) collective-permute-start(bf16[2,128,512]{1,2,0:T(8,128)(2,1)} %collective-permute-done), channel_id=1, source_target_pairs={{0,1},{1,2},{2,3},{3,4},{4,5},{5,6},{6,7},{7,8},{8,9},{9,10},{10,1... | collective-permute-start | bytes 786440 | tf_op jit(solution)/shard_map/ppermute | solution.py:17
  37.5 2.0 %fusion.26 = f32[4,128,128,1]{1,2,3,0:T(8,128)S(1)} fusion(bf16[128,4,8,128]{0,3,2,1:T(8,128)(2,1)S(1)} %copy.214, f32[4,8,128,128]{2,3,1,0:T(8,128)} %copy-done.2), kind=kOutput, calls=%fused_computation.42 | convolution fusion | flops 134742016 | bytes 3407872 | tf_op jit(solution)/shard_map/kgts,tkgd->skd/dot_general | solution.py:71
  41.1 1.0 fusion.40
  42.1 1.3 %fusion.15 = f32[4,8,128,128]{2,3,1,0:T(8,128)S(1)} fusion(bf16[128,4,128,1]{0,2,3,1:T(8,128)(2,1)S(1)} %bitcast.282, bf16[128,4,8,128]{0,3,2,1:T(8,128)(2,1)S(1)} %bitcast.270, f32[4,8,128]{2,1,0:T(8,128)} %bitcast.309, pred[128,128]{0,1:T(8,128)(4,1)} %get-tuple-element.31), kind=kOutput, calls=%fused_computation.24 | convolution fusion | flops 135790592 | bytes 3309568 | tf_op jit(solution)/shard_map/tkgd,skd->kgts/dot_general | solution.py:54
  43.4 5.3 %collective-permute-start.2 = (bf16[2,128,512]{1,2,0:T(8,128)(2,1)}, bf16[2,128,512]{1,2,0:T(8,128)(2,1)S(1)}, u32[]{:S(2)}, u32[]{:S(2)}) collective-permute-start(bf16[2,128,512]{1,2,0:T(8,128)(2,1)} %collective-permute-done.1), channel_id=1, source_target_pairs={{0,1},{1,2},{2,3},{3,4},{4,5},{5,6},{6,7},{7,8},{8,9},{9,10},{10,1... | collective-permute-start | bytes 786440 | tf_op jit(solution)/shard_map/ppermute | solution.py:17
  48.7 1.5 %fusion.13 = bf16[4,8,128,128]{2,3,1,0:T(8,128)(2,1)} fusion(f32[4,8,128,128]{2,3,1,0:T(8,128)S(1)} %fusion.15, bf16[128,4,128,1]{0,2,3,1:T(8,128)(2,1)S(1)} %bitcast.302, bf16[128,4,8,128]{0,3,2,1:T(8,128)(2,1)S(1)} %copy.214, f32[4,8,128]{2,1,0:T(8,128)S(1)} %copy.186), kind=kOutput, calls=%fused_computation.21 | convolution fusion | flops 136314880 | bytes 4341760 | tf_op jit(solution)/shard_map/tkgd,skd->kgts/dot_general | solution.py:61
  50.3 2.1 %collective-permute-done.2 = bf16[2,128,512]{1,2,0:T(8,128)(2,1)S(1)} collective-permute-done((bf16[2,128,512]{1,2,0:T(8,128)(2,1)}, bf16[2,128,512]{1,2,0:T(8,128)(2,1)S(1)}, u32[]{:S(2)}, u32[]{:S(2)}) %collective-permute-start.2) | collective-permute-done | bytes 262176 | tf_op jit(solution)/shard_map/ppermute | solution.py:17
  53.0 5.2 %collective-permute-start.3 = (bf16[2,128,512]{1,2,0:T(8,128)(2,1)S(1)}, bf16[2,128,512]{1,2,0:T(8,128)(2,1)S(1)}, u32[]{:S(2)}, u32[]{:S(2)}) collective-permute-start(bf16[2,128,512]{1,2,0:T(8,128)(2,1)S(1)} %collective-permute-done.2), channel_id=1, source_target_pairs={{0,1},{1,2},{2,3},{3,4},{4,5},{5,6},{6,7},{7,8},{8,9},{9,10},{10,1... | collective-permute-start | bytes 786440 | tf_op jit(solution)/shard_map/ppermute | solution.py:17
  58.2 1.5 %fusion.8 = bf16[4,8,128,128]{2,3,1,0:T(8,128)(2,1)} fusion(f32[4,8,128,128]{2,3,1,0:T(8,128)S(1)} %fusion.10, bf16[128,4,128,1]{0,2,3,1:T(8,128)(2,1)S(1)} %bitcast.303, bf16[128,4,8,128]{0,3,2,1:T(8,128)(2,1)S(1)} %copy.214, f32[4,8,128]{2,1,0:T(8,128)S(1)} %copy.186), kind=kOutput, calls=%fused_computation.13 | convolution fusion | flops 136314880 | bytes 4341760 | tf_op jit(solution)/shard_map/tkgd,skd->kgts/dot_general | solution.py:61
  59.7 1.8 %collective-permute-done.3 = bf16[2,128,512]{1,2,0:T(8,128)(2,1)S(1)} collective-permute-done((bf16[2,128,512]{1,2,0:T(8,128)(2,1)S(1)}, bf16[2,128,512]{1,2,0:T(8,128)(2,1)S(1)}, u32[]{:S(2)}, u32[]{:S(2)}) %collective-permute-start.3) | collective-permute-done | bytes 262176 | tf_op jit(solution)/shard_map/ppermute | solution.py:17
  62.8 1.2 fusion.32
  64.5 1.0 copy-done.5
  65.5 1.2 fusion.46
  66.7 1.8 %copy.221 = f32[1,128,512]{2,1,0:T(8,128)} copy(f32[1,128,512]{1,2,0:T(8,128)} %bitcast.291) | data formatting | bytes 524288 | tf_op jit(solution)/shard_map/stack;reshape | solution.py:74
  68.5 1.8 %copy.222 = f32[1,128,512]{2,1,0:T(8,128)} copy(f32[1,128,512]{1,2,0:T(8,128)} %bitcast.294) | data formatting | bytes 524288 | tf_op jit(solution)/shard_map/stack;reshape | solution.py:74
  70.3 1.9 %pad_maximum_fusion = f32[2,128,512]{2,1,0:T(8,128)} fusion(f32[1,128,512]{2,1,0:T(8,128)} %copy.222, f32[1,128,512]{2,1,0:T(8,128)} %copy.221), kind=kLoop, calls=%fused_computation.54 | loop fusion | flops 131072 | bytes 1048576 | tf_op jit(solution)/shard_map/stack | solution.py:74
  72.2 2.1 %collective-permute-start.4 = (f32[2,128,512]{2,1,0:T(8,128)}, f32[2,128,512]{2,1,0:T(8,128)}, u32[]{:S(2)}, u32[]{:S(2)}) collective-permute-start(f32[2,128,512]{2,1,0:T(8,128)} %pad_maximum_fusion), channel_id=1, source_target_pairs={{1,0},{2,1},{3,2},{4,3},{5,4},{6,5},{7,6},{8,7},{9,8},{10,9},{11,1... | collective-permute-start | bytes 1572872 | tf_op jit(solution)/shard_map/ppermute | solution.py:17
  74.3 2.4 %fusion.47 = f32[4,128,128,1]{1,2,3,0:T(8,128)} fusion(bf16[4,8,128,128]{2,3,1,0:T(8,128)(2,1)} %fusion.8, bf16[128,4,8,128]{0,3,2,1:T(8,128)(2,1)S(1)} %bitcast.274), kind=kOutput, calls=%fused_computation.91 | convolution fusion | flops 134217728 | bytes 2359296 | tf_op jit(solution)/shard_map/kgts,tkgd->skd/dot_general | solution.py:68
  76.6 1.8 %copy.227 = f32[1,128,512]{2,1,0:T(8,128)} copy(f32[1,128,512]{1,2,0:T(8,128)} %bitcast.292) | data formatting | bytes 524288 | tf_op jit(solution)/shard_map/stack;reshape | solution.py:74
  78.4 2.7 %fusion.30 = f32[4,128,128,1]{1,2,3,0:T(8,128)} fusion(bf16[128,4,8,128]{0,3,2,1:T(8,128)(2,1)S(1)} %copy.214, f32[4,8,128,128]{2,3,1,0:T(8,128)} %copy-done.1), kind=kOutput, calls=%fused_computation.46 | convolution fusion | flops 134742016 | bytes 3407872 | tf_op jit(solution)/shard_map/kgts,tkgd->skd/dot_general | solution.py:71
  81.2 1.8 %copy.228 = f32[1,128,512]{2,1,0:T(8,128)} copy(f32[1,128,512]{1,2,0:T(8,128)} %bitcast.299) | data formatting | bytes 524288 | tf_op jit(solution)/shard_map/stack;reshape | solution.py:74
  83.0 1.6 %collective-permute-done.4 = f32[2,128,512]{2,1,0:T(8,128)} collective-permute-done((f32[2,128,512]{2,1,0:T(8,128)}, f32[2,128,512]{2,1,0:T(8,128)}, u32[]{:S(2)}, u32[]{:S(2)}) %collective-permute-start.4) | collective-permute-done | bytes 524320 | tf_op jit(solution)/shard_map/ppermute | solution.py:17
  84.6 2.1 %maximum_add_fusion.1 = f32[2,128,512]{2,1,0:T(8,128)} fusion(f32[2,128,512]{2,1,0:T(8,128)} %collective-permute-done.4, f32[1,128,512]{2,1,0:T(8,128)} %copy.228, f32[1,128,512]{2,1,0:T(8,128)} %copy.227), kind=kLoop, calls=%fused_computation.55 | loop fusion | flops 262144 | bytes 1572864 | tf_op jit(solution)/shard_map/add | solution.py:87
  86.7 1.9 %collective-permute-start.5 = (f32[2,128,512]{2,1,0:T(8,128)}, f32[2,128,512]{2,1,0:T(8,128)}, u32[]{:S(2)}, u32[]{:S(2)}) collective-permute-start(f32[2,128,512]{2,1,0:T(8,128)} %maximum_add_fusion.1), channel_id=1, source_target_pairs={{1,0},{2,1},{3,2},{4,3},{5,4},{6,5},{7,6},{8,7},{9,8},{10,9},{11,1... | collective-permute-start | bytes 1572872 | tf_op jit(solution)/shard_map/ppermute | solution.py:17
  88.6 2.4 %fusion.48 = f32[4,128,128,1]{1,2,3,0:T(8,128)} fusion(bf16[4,8,128,128]{2,3,1,0:T(8,128)(2,1)} %fusion.13, bf16[128,4,8,128]{0,3,2,1:T(8,128)(2,1)S(1)} %bitcast.275), kind=kOutput, calls=%fused_computation.92 | convolution fusion | flops 134217728 | bytes 2359296 | tf_op jit(solution)/shard_map/kgts,tkgd->skd/dot_general | solution.py:68
  91.0 1.1 copy.233
  92.1 2.0 %fusion.28 = f32[4,128,128,1]{1,2,3,0:T(8,128)S(1)} fusion(bf16[128,4,8,128]{0,3,2,1:T(8,128)(2,1)S(1)} %copy.214, f32[4,8,128,128]{2,3,1,0:T(8,128)} %copy-done), kind=kOutput, calls=%fused_computation.44 | convolution fusion | flops 134742016 | bytes 3407872 | tf_op jit(solution)/shard_map/kgts,tkgd->skd/dot_general | solution.py:71
  94.3 4.1 %collective-permute-done.5 = f32[2,128,512]{2,1,0:T(8,128)} collective-permute-done((f32[2,128,512]{2,1,0:T(8,128)}, f32[2,128,512]{2,1,0:T(8,128)}, u32[]{:S(2)}, u32[]{:S(2)}) %collective-permute-start.5) | collective-permute-done | bytes 524320 | tf_op jit(solution)/shard_map/ppermute | solution.py:17
  98.4 1.1 maximum_add_fusion.2
  99.5 1.9 %collective-permute-start.6 = (f32[2,128,512]{2,1,0:T(8,128)S(1)}, f32[2,128,512]{2,1,0:T(8,128)S(1)}, u32[]{:S(2)}, u32[]{:S(2)}) collective-permute-start(f32[2,128,512]{2,1,0:T(8,128)S(1)} %maximum_add_fusion.2), channel_id=1, source_target_pairs={{1,0},{2,1},{3,2},{4,3},{5,4},{6,5},{7,6},{8,7},{9,8},{10,9},{11,1... | collective-permute-start | bytes 1572872 | tf_op jit(solution)/shard_map/ppermute | solution.py:17
  102.4 8.5 %collective-permute-done.6 = f32[2,128,512]{2,1,0:T(8,128)S(1)} collective-permute-done((f32[2,128,512]{2,1,0:T(8,128)S(1)}, f32[2,128,512]{2,1,0:T(8,128)S(1)}, u32[]{:S(2)}, u32[]{:S(2)}) %collective-permute-start.6) | collective-permute-done | bytes 524320 | tf_op jit(solution)/shard_map/ppermute | solution.py:17
  111.0 1.9 %collective-permute-start.7 = (f32[2,128,512]{2,1,0:T(8,128)S(1)}, f32[2,128,512]{2,1,0:T(8,128)S(1)}, u32[]{:S(2)}, u32[]{:S(2)}) collective-permute-start(f32[2,128,512]{2,1,0:T(8,128)S(1)} %maximum_add_fusion.3), channel_id=1, source_target_pairs={{1,0},{2,1},{3,2},{4,3},{5,4},{6,5},{7,6},{8,7},{9,8},{10,9},{11,1... | collective-permute-start | bytes 1572872 | tf_op jit(solution)/shard_map/ppermute | solution.py:17
  114.2 1.3 %copy.241 = bf16[128,4096]{1,0:T(8,128)(2,1)} copy(bf16[128,4096]{0,1:T(8,128)(2,1)S(1)} %bitcast.279) | data formatting | bytes 2097152
  115.5 6.9 %collective-permute-done.7 = f32[2,128,512]{2,1,0:T(8,128)S(1)} collective-permute-done((f32[2,128,512]{2,1,0:T(8,128)S(1)}, f32[2,128,512]{2,1,0:T(8,128)S(1)}, u32[]{:S(2)}, u32[]{:S(2)}) %collective-permute-start.7) | collective-permute-done | bytes 524320 | tf_op jit(solution)/shard_map/ppermute | solution.py:17
  (76 shorter events, 20.7 us)
Async XLA Ops:
  0.6 12.7 %copy-start.12 = (bf16[128,4096]{1,0:T(8,128)(2,1)S(1)}, bf16[128,4096]{1,0:T(8,128)(2,1)}, u32[]{:S(2)}) copy-start(bf16[128,4096]{1,0:T(8,128)(2,1)} %param.7) | copy-start | bytes 3145732
  3.5 27.8 %collective-permute-start = (bf16[2,128,512]{1,2,0:T(8,128)(2,1)}, bf16[2,128,512]{1,2,0:T(8,128)(2,1)}, u32[]{:S(2)}, u32[]{:S(2)}) collective-permute-start(bf16[2,128,512]{1,2,0:T(8,128)(2,1)} %pad_maximum_fusion.1), channel_id=1, source_target_pairs={{0,1},{1,2},{2,3},{3,4},{4,5},{5,6},{6,7},{7,8},{8,9},{9,10},{10,1... | collective-permute-start | bytes 786440 | tf_op jit(solution)/shard_map/ppermute | solution.py:17
  27.8 4.6 %copy-start.15 = (f32[32,128]{1,0:T(8,128)S(1)}, f32[32,128]{1,0:T(8,128)}, u32[]{:S(2)}) copy-start(f32[32,128]{1,0:T(8,128)} %param.12) | copy-start | bytes 49156
  27.8 4.6 %copy-start.19 = (pred[128,128]{0,1:T(8,128)(4,1)S(1)}, pred[128,128]{0,1:T(8,128)(4,1)}, u32[]{:S(2)}) copy-start(pred[128,128]{0,1:T(8,128)(4,1)} %get-tuple-element.33) | copy-start | bytes 49156
  33.0 1.3 %copy-start.2 = (f32[4,8,128,128]{2,3,1,0:T(8,128)}, f32[4,8,128,128]{2,3,1,0:T(8,128)S(1)}, u32[]{:S(2)}) copy-start(f32[4,8,128,128]{2,3,1,0:T(8,128)S(1)} %fusion.20) | copy-start | bytes 6291460
  35.6 5.5 %collective-permute-start.1 = (bf16[2,128,512]{1,2,0:T(8,128)(2,1)}, bf16[2,128,512]{1,2,0:T(8,128)(2,1)}, u32[]{:S(2)}, u32[]{:S(2)}) collective-permute-start(bf16[2,128,512]{1,2,0:T(8,128)(2,1)} %collective-permute-done), channel_id=1, source_target_pairs={{0,1},{1,2},{2,3},{3,4},{4,5},{5,6},{6,7},{7,8},{8,9},{9,10},{10,1... | collective-permute-start | bytes 786440 | tf_op jit(solution)/shard_map/ppermute | solution.py:17
  43.4 6.8 %copy-start = (f32[4,8,128,128]{2,3,1,0:T(8,128)}, f32[4,8,128,128]{2,3,1,0:T(8,128)S(1)}, u32[]{:S(2)}) copy-start(f32[4,8,128,128]{2,3,1,0:T(8,128)S(1)} %fusion.15) | copy-start | bytes 6291460
  43.4 8.9 %collective-permute-start.2 = (bf16[2,128,512]{1,2,0:T(8,128)(2,1)}, bf16[2,128,512]{1,2,0:T(8,128)(2,1)S(1)}, u32[]{:S(2)}, u32[]{:S(2)}) collective-permute-start(bf16[2,128,512]{1,2,0:T(8,128)(2,1)} %collective-permute-done.1), channel_id=1, source_target_pairs={{0,1},{1,2},{2,3},{3,4},{4,5},{5,6},{6,7},{7,8},{8,9},{9,10},{10,1... | collective-permute-start | bytes 786440 | tf_op jit(solution)/shard_map/ppermute | solution.py:17
  48.7 3.6 %copy-start.16 = (f32[32,128]{1,0:T(8,128)S(1)}, f32[32,128]{1,0:T(8,128)}, u32[]{:S(2)}) copy-start(f32[32,128]{1,0:T(8,128)} %param.12) | copy-start | bytes 49156
  48.7 3.6 %copy-start.18 = (pred[128,128]{0,1:T(8,128)(4,1)S(1)}, pred[128,128]{0,1:T(8,128)(4,1)}, u32[]{:S(2)}) copy-start(pred[128,128]{0,1:T(8,128)(4,1)} %get-tuple-element.32) | copy-start | bytes 49156
  53.0 6.7 %copy-start.1 = (f32[4,8,128,128]{2,3,1,0:T(8,128)}, f32[4,8,128,128]{2,3,1,0:T(8,128)S(1)}, u32[]{:S(2)}) copy-start(f32[4,8,128,128]{2,3,1,0:T(8,128)S(1)} %fusion.10) | copy-start | bytes 6291460
  53.0 8.5 %collective-permute-start.3 = (bf16[2,128,512]{1,2,0:T(8,128)(2,1)S(1)}, bf16[2,128,512]{1,2,0:T(8,128)(2,1)S(1)}, u32[]{:S(2)}, u32[]{:S(2)}) collective-permute-start(bf16[2,128,512]{1,2,0:T(8,128)(2,1)S(1)} %collective-permute-done.2), channel_id=1, source_target_pairs={{0,1},{1,2},{2,3},{3,4},{4,5},{5,6},{6,7},{7,8},{8,9},{9,10},{10,1... | collective-permute-start | bytes 786440 | tf_op jit(solution)/shard_map/ppermute | solution.py:17
  58.2 4.0 %copy-start.17 = (pred[128,128]{0,1:T(8,128)(4,1)S(1)}, pred[128,128]{0,1:T(8,128)(4,1)}, u32[]{:S(2)}) copy-start(pred[128,128]{0,1:T(8,128)(4,1)} %get-tuple-element.30) | copy-start | bytes 49156
  61.5 0.7 copy-start.8
  64.5 1.0 copy-start.5
  72.2 12.5 %collective-permute-start.4 = (f32[2,128,512]{2,1,0:T(8,128)}, f32[2,128,512]{2,1,0:T(8,128)}, u32[]{:S(2)}, u32[]{:S(2)}) collective-permute-start(f32[2,128,512]{2,1,0:T(8,128)} %pad_maximum_fusion), channel_id=1, source_target_pairs={{1,0},{2,1},{3,2},{4,3},{5,4},{6,5},{7,6},{8,7},{9,8},{10,9},{11,1... | collective-permute-start | bytes 1572872 | tf_op jit(solution)/shard_map/ppermute | solution.py:17
  86.7 11.7 %collective-permute-start.5 = (f32[2,128,512]{2,1,0:T(8,128)}, f32[2,128,512]{2,1,0:T(8,128)}, u32[]{:S(2)}, u32[]{:S(2)}) collective-permute-start(f32[2,128,512]{2,1,0:T(8,128)} %maximum_add_fusion.1), channel_id=1, source_target_pairs={{1,0},{2,1},{3,2},{4,3},{5,4},{6,5},{7,6},{8,7},{9,8},{10,9},{11,1... | collective-permute-start | bytes 1572872 | tf_op jit(solution)/shard_map/ppermute | solution.py:17
  94.3 7.6 %copy-start.3 = (bf16[4,8,128,128]{2,3,1,0:T(8,128)(2,1)S(1)}, bf16[4,8,128,128]{2,3,1,0:T(8,128)(2,1)}, u32[]{:S(2)}) copy-start(bf16[4,8,128,128]{2,3,1,0:T(8,128)(2,1)} %fusion.13) | copy-start | bytes 3145732
  99.5 11.4 %collective-permute-start.6 = (f32[2,128,512]{2,1,0:T(8,128)S(1)}, f32[2,128,512]{2,1,0:T(8,128)S(1)}, u32[]{:S(2)}, u32[]{:S(2)}) collective-permute-start(f32[2,128,512]{2,1,0:T(8,128)S(1)} %maximum_add_fusion.2), channel_id=1, source_target_pairs={{1,0},{2,1},{3,2},{4,3},{5,4},{6,5},{7,6},{8,7},{9,8},{10,9},{11,1... | collective-permute-start | bytes 1572872 | tf_op jit(solution)/shard_map/ppermute | solution.py:17
  101.9 9.0 %copy-start.13 = (f32[1,128,512]{2,1,0:T(8,128)S(1)}, f32[1,128,512]{2,1,0:T(8,128)}, u32[]{:S(2)}) copy-start(f32[1,128,512]{2,1,0:T(8,128)} %copy.239) | copy-start | bytes 786436
  101.9 9.0 %copy-start.14 = (f32[1,128,512]{2,1,0:T(8,128)S(1)}, f32[1,128,512]{2,1,0:T(8,128)}, u32[]{:S(2)}) copy-start(f32[1,128,512]{2,1,0:T(8,128)} %copy.240) | copy-start | bytes 786436
  101.9 11.0 %copy-start.4 = (bf16[4,8,128,128]{2,3,1,0:T(8,128)(2,1)S(1)}, bf16[4,8,128,128]{2,3,1,0:T(8,128)(2,1)}, u32[]{:S(2)}) copy-start(bf16[4,8,128,128]{2,3,1,0:T(8,128)(2,1)} %fusion.8) | copy-start | bytes 3145732
  102.4 11.0 %copy-start.6 = (bf16[4,8,128,128]{2,3,1,0:T(8,128)(2,1)S(1)}, bf16[4,8,128,128]{2,3,1,0:T(8,128)(2,1)}, u32[]{:S(2)}) copy-start(bf16[4,8,128,128]{2,3,1,0:T(8,128)(2,1)} %copy-done.5) | copy-start | bytes 3145732
  102.4 11.0 %copy-start.7 = (f32[4,8,128,128]{2,3,1,0:T(8,128)S(1)}, f32[4,8,128,128]{2,3,1,0:T(8,128)}, u32[]{:S(2)}) copy-start(f32[4,8,128,128]{2,3,1,0:T(8,128)} %fusion.50) | copy-start | bytes 6291460
  102.4 11.0 %copy-start.9 = (bf16[1,128,512]{1,2,0:T(8,128)(2,1)S(1)}, bf16[1,128,512]{1,2,0:T(8,128)(2,1)}, u32[]{:S(2)}) copy-start(bf16[1,128,512]{1,2,0:T(8,128)(2,1)} %copy-done.8) | copy-start | bytes 393220
  111.0 11.4 %collective-permute-start.7 = (f32[2,128,512]{2,1,0:T(8,128)S(1)}, f32[2,128,512]{2,1,0:T(8,128)S(1)}, u32[]{:S(2)}, u32[]{:S(2)}) collective-permute-start(f32[2,128,512]{2,1,0:T(8,128)S(1)} %maximum_add_fusion.3), channel_id=1, source_target_pairs={{1,0},{2,1},{3,2},{4,3},{5,4},{6,5},{7,6},{8,7},{9,8},{10,9},{11,1... | collective-permute-start | bytes 1572872 | tf_op jit(solution)/shard_map/ppermute | solution.py:17
  114.2 8.3 %copy-start.10 = (f32[1,128,512]{2,1,0:T(8,128)S(1)}, f32[1,128,512]{2,1,0:T(8,128)}, u32[]{:S(2)}) copy-start(f32[1,128,512]{2,1,0:T(8,128)} %copy.215) | copy-start | bytes 786436
  114.2 8.3 %copy-start.11 = (f32[1,128,512]{2,1,0:T(8,128)S(1)}, f32[1,128,512]{2,1,0:T(8,128)}, u32[]{:S(2)}) copy-start(f32[1,128,512]{2,1,0:T(8,128)} %copy.216) | copy-start | bytes 786436
where the time goes:
time: 124 us; the launch traced here: 123 us
  local copies, waits for them, and re-layouts  28.6 us (23%)
  matrix products  28.6 us (23%)
  waiting for transfers between devices  25.8 us (21%)
  starting transfers between devices  24 us (19%)
  other arithmetic  15.1 us (12%)
    ppermute x8, waiting for transfers between devices, shifted(): return lax.ppermute(block, axis, route)  25.8 us
    ppermute x8, starting transfers between devices, shifted(): return lax.ppermute(block, axis, route)  24 us
    another operation x10, local copies, waits for them, and re-layouts, attend(): return (query_part, jnp.stack([key_part, value_part]))  12.7 us
    dot_general x5, matrix products, attend(): jnp.einsum('kgts,tkgd->skd', weights_low, gradient_per_head, preferred_el...  9.13 us
    unnamed x45, local copies, waits for them, and re-layouts  7.8 us
    dot_general x5, matrix products, attend(): jnp.einsum('kgts,tkgd->skd', grad_score, query_per_head, preferred_elemen...  6.77 us
    dot_general x5, matrix products, attend(): jnp.einsum('tkgd,skd->kgts', gradient_per_head, value_tile, preferred_ele...  4.53 us
    dot_general x5, matrix products, attend(): jnp.einsum('tkgd,skd->kgts', query_per_head, key_tile, preferred_element_...  4.44 us
  transfers between devices with their start and end apart: 8, of which 7 were waited for; matrix products, arithmetic and copies ran while one was open for 39% of the time, Pallas kernels for 0%

commit v1 on v0

v1 whole, which is shorter than its diff:
```python
import functools
import math

import jax
import jax.numpy as jnp
from jax import lax
from jax.experimental import pallas as pl
from jax.experimental.pallas import tpu as pltpu
from jax.sharding import PartitionSpec as P

HD = 128
KVH = 4
SPAN = 4
LOG2E = 1.0 / math.log(2.0)
MESH = pl.DeviceIdType.MESH
F32 = jnp.float32
BF16 = jnp.bfloat16

CX, C, X, PB, M = range(5)


def nt(a, b):
    return lax.dot_general(a, b, (((1,), (1,)), ((), ())), preferred_element_type=F32)


def nn(a, b):
    return jnp.dot(a, b, preferred_element_type=F32)


def kernel(
    n, docs,
    doc_ref, q_hbm, k_hbm, v_hbm, o_hbm, do_hbm, ln_hbm,
    dq_hbm, dk_ref, dv_ref,
    q, o, do, ln, own, dq, kv, bias, rd, wbuf, gbuf, kt, acc_x, acc, bsend, brecv,
    load_sem, store_sem, fs_sem, fr_sem, bs_sem, br_sem,
):
    T = q_hbm.shape[0]
    heads = q_hbm.shape[1] // HD
    group = heads // KVH
    wide = group * HD
    inv_root = 1.0 / math.sqrt(HD)
    me = lax.axis_index("ctx")
    place = lax.rem(me, 4)
    x = place // 2
    c = lax.rem(place, 2)
    mate = me + 1 - 2 * c
    peer = me + 2 - 4 * x
    after = me + SPAN
    before = me - SPAN
    has_after = after < n
    has_before = before >= 0

    def load(i, src, dst):
        return pltpu.make_async_copy(src, dst, load_sem.at[i])

    loads_kv = [load(0, k_hbm, own.at[0]), load(1, v_hbm, own.at[1])]
    loads_rd = [load(2, do_hbm, do), load(3, o_hbm, o)]
    loads_q = [load(4, q_hbm, q), load(5, ln_hbm, ln)]
    for cp in loads_kv + loads_rd + loads_q:
        cp.start()

    barrier = pltpu.get_barrier_semaphore()
    pl.semaphore_signal(barrier, inc=1, device_id={"ctx": mate}, device_id_type=MESH)
    pl.semaphore_signal(barrier, inc=1, device_id={"ctx": peer}, device_id_type=MESH)

    @pl.when(has_after)
    def _():
        pl.semaphore_signal(barrier, inc=1, device_id={"ctx": after}, device_id_type=MESH)

    @pl.when(has_before)
    def _():
        pl.semaphore_signal(barrier, inc=1, device_id={"ctx": before}, device_id_type=MESH)

    for cp in loads_kv:
        cp.wait()
    for g in range(KVH):
        for a in range(2):
            kv[g, a, M * T:(M + 1) * T, :] = own[a, :, g * HD:(g + 1) * HD]

    @pl.when(jnp.logical_not(has_before))
    def _():
        kv[:, :, PB * T:(PB + 1) * T, :] = jnp.zeros((KVH, 2, T, HD), BF16)

    wait_for = 2 + jnp.where(has_after, 1, 0) + jnp.where(has_before, 1, 0)
    pl.semaphore_wait(barrier, wait_for)

    def fwd(kind, g, slot, target):
        row = slot * T if isinstance(slot, int) else pl.multiple_of(slot * T, T)
        return pltpu.make_async_remote_copy(
            src_ref=kv.at[g, :, pl.ds(row, T), :],
            dst_ref=kv.at[g, :, pl.ds(kind * T, T), :],
            send_sem=fs_sem.at[kind, g], recv_sem=fr_sem.at[kind, g],
            device_id={"ctx": target}, device_id_type=MESH,
        )

    def fwd_p(g):
        return fwd(PB, g, M, after)

    def fwd_x(g):
        return fwd(X, g, M - x, peer)

    def fwd_c(g):
        return fwd(C, g, M - c, mate)

    def fwd_cx(g):
        return fwd(CX, g, X, mate)

    @pl.when(has_after)
    def _():
        for g in range(KVH):
            fwd_p(g).start()

    @pl.when(x == 0)
    def _():
        for g in range(KVH):
            fwd_x(g).start()

    @pl.when(c == 0)
    def _():
        for g in range(KVH):
            fwd_c(g).start()

    def relay_p(g):
        @pl.when(has_before)
        def _():
            fwd_p(g).wait_recv()

        @pl.when(x == 1)
        def _():
            fwd_x(g).start()

        @pl.when(c == 1)
        def _():
            fwd_c(g).start()

    def relay_x(g):
        fwd_x(g).wait_recv()
        fwd_cx(g).start()

    def arrived(g):
        fwd_c(g).wait_recv()
        fwd_cx(g).wait_recv()

    t_row = lax.broadcasted_iota(jnp.int32, (1, T), 1)
    pos_row = me * T + t_row
    start_row = jnp.zeros((1, T), jnp.int32)
    end = jnp.int32(0)
    for i in range(docs):
        end = end + doc_ref[i]
        start_row = jnp.where(end <= pos_row, jnp.maximum(start_row, end), start_row)
    s_col = lax.broadcasted_iota(jnp.int32, (T, T), 0)
    t_col = lax.broadcasted_iota(jnp.int32, (T, T), 1)
    tri1 = s_col <= t_col
    bases = (me - 1 - 2 * c, me - 3 + 2 * c, me - 2)
    for slot, base in enumerate(bases):
        ok = base * T + s_col >= start_row
        b = jnp.where(ok, 0.0, -1e30).astype(F32)
        bias[slot * T:(slot + 1) * T, :] = b
    ok = jnp.where(tri1, me, me - SPAN) * T + s_col >= start_row
    bias[3 * T:4 * T, :] = jnp.where(ok, 0.0, -1e30).astype(F32)

    for cp in loads_rd:
        cp.wait()
    pick = (
        lax.broadcasted_iota(jnp.int32, (16, wide), 1) // HD
        == lax.broadcasted_iota(jnp.int32, (16, wide), 0)
    )
    ones = jnp.where(pick, 1.0, 0.0).astype(BF16)
    for g in range(KVH):
        cols = slice(g * wide, (g + 1) * wide)
        prod = do[:, cols].astype(F32) * o[:, cols].astype(F32)
        high = prod.astype(BF16)
        low = (prod - high.astype(F32)).astype(BF16)
        rd[g * group:(g + 1) * group, :] = (nt(ones, high) + nt(ones, low))[:group]
    for cp in loads_q:
        cp.wait()

    relay_p(0)
    relay_x(0)
    relay_p(1)

    def bwd(kind, g, target):
        return pltpu.make_async_remote_copy(
            src_ref=bsend.at[kind, g], dst_ref=brecv.at[kind, g],
            send_sem=bs_sem.at[kind, g], recv_sem=br_sem.at[kind, g],
            device_id={"ctx": target}, device_id_type=MESH,
        )

    def store(g):
        cols = pl.ds(g * wide, wide)
        return pltpu.make_async_copy(dq.at[:, cols], dq_hbm.at[:, cols], store_sem.at[g])

    def hop2(g):
        bwd(CX, g, mate).wait_recv()
        bsend[X, g] = (acc_x[g] + brecv[CX, g].astype(F32)).astype(BF16)
        bwd(X, g, peer).start()

    def hop3(g):
        bwd(C, g, mate).wait_recv()
        acc[c, g] = acc[c, g] + brecv[C, g].astype(F32)
        bwd(X, g, peer).wait_recv()
        acc[x, g] = acc[x, g] + brecv[X, g].astype(F32)

        @pl.when(has_before)
        def _():
            bsend[PB, g] = acc[1, g].astype(BF16)
            bwd(PB, g, before).start()

    def hop4(g):
        cols = slice(g * HD, (g + 1) * HD)

        @pl.when(has_after)
        def _():
            bwd(PB, g, before).wait_recv()
            total = acc[0, g] + brecv[PB, g].astype(F32)
            dk_ref[:, cols] = total[0].astype(BF16)
            dv_ref[:, cols] = total[1].astype(BF16)

        @pl.when(jnp.logical_not(has_after))
        def _():
            dk_ref[:, cols] = acc[0, g, 0].astype(BF16)
            dv_ref[:, cols] = acc[0, g, 1].astype(BF16)

    def pair_rows(ref, h):
        return jnp.concatenate(
            [ref[:, h * HD:(h + 1) * HD], ref[:, (h + 1) * HD:(h + 2) * HD]], axis=0
        )

    def pair_lanes(ref, h):
        return jnp.concatenate([ref[h:h + 1, :], ref[h + 1:h + 2, :]], axis=1)

    def scores(g, between):
        k_all = kv[g, 0]
        v_all = kv[g, 1]
        kt[...] = k_all.T
        tri = jnp.concatenate([tri1, tri1], axis=1)
        for p in range(group // 2):
            h = g * group + 2 * p
            st = nt(k_all, pair_rows(q, h))
            gp = nt(v_all, pair_rows(do, h))
            shift = pair_lanes(ln, h) * LOG2E
            dot_row = pair_lanes(rd, h)
            lanes = slice(p * 2 * T, (p + 1) * 2 * T)
            for slot in range(4):
                rows = slice(slot * T, (slot + 1) * T)
                s_t, g_t = st[rows], gp[rows]
                if slot == 3:
                    s_t = jnp.where(tri, st[M * T:], s_t)
                    g_t = jnp.where(tri, gp[M * T:], g_t)
                b = bias[rows, :]
                b = jnp.concatenate([b, b], axis=1)
                w = jnp.exp2(s_t * (inv_root * LOG2E) - shift + b)
                gs = w * (g_t - dot_row)
                if slot == 3:
                    wbuf[M * T:, lanes] = jnp.where(tri, w, 0.0).astype(BF16)
                    gbuf[M * T:, lanes] = jnp.where(tri, gs, 0.0).astype(BF16)
                    w = jnp.where(tri, 0.0, w)
                    gs = jnp.where(tri, 0.0, gs)
                wbuf[rows, lanes] = w.astype(BF16)
                gbuf[rows, lanes] = gs.astype(BF16)
            dqt = nn(kt[...], gbuf[:, lanes]) * inv_root
            dq[:, h * HD:(h + 1) * HD] = dqt[:, :T].T.astype(BF16)
            dq[:, (h + 1) * HD:(h + 2) * HD] = dqt[:, T:].T.astype(BF16)
            between(p)

    def stacked(ref, g):
        return jnp.concatenate(
            [ref[:, (g * group + i) * HD:(g * group + i + 1) * HD] for i in range(group)], axis=0
        )

    for g in range(KVH):
        if g > 0:
            relay_x(g)
            if g + 1 < KVH:
                relay_p(g + 1)
        arrived(g)

        def between(p, g=g):
            if p == 1 and g >= 1:
                hop2(g - 1)
            if p == 3 and g >= 1:
                hop3(g - 1)

        scores(g, between)
        store(g).start()
        dk = nn(gbuf[...], stacked(q, g)) * inv_root
        dv = nn(wbuf[...], stacked(do, g))
        for kind in (CX, C):
            bsend[kind, g, 0] = dk[kind * T:(kind + 1) * T].astype(BF16)
            bsend[kind, g, 1] = dv[kind * T:(kind + 1) * T].astype(BF16)
            bwd(kind, g, mate).start()
        for a, part in enumerate((dk, dv)):
            acc_x[g, a] = part[X * T:(X + 1) * T]
            acc[1, g, a] = part[PB * T:(PB + 1) * T]
            acc[0, g, a] = part[M * T:]
    hop2(KVH - 1)
    for g in range(KVH - 1):
        hop4(g)
    hop3(KVH - 1)
    hop4(KVH - 1)

    for g in range(KVH):
        store(g).wait()
        for kind, target in ((CX, mate), (C, mate), (X, peer)):
            bwd(kind, g, target).wait_send()
        fwd_x(g).wait_send()
        fwd_c(g).wait_send()
        fwd_cx(g).wait_send()

    @pl.when(has_after)
    def _():
        for g in range(KVH):
            fwd_p(g).wait_send()

    @pl.when(has_before)
    def _():
        for g in range(KVH):
            bwd(PB, g, before).wait_send()


def body(n, queries, keys, values, outputs, out_grad, log_normalizer, doc_lengths):
    T, width = queries.shape
    heads = width // HD
    group = heads // KVH
    any_spec = pl.BlockSpec(memory_space=pl.ANY)
    vmem = pl.BlockSpec(memory_space=pltpu.VMEM)
    dma = pltpu.SemaphoreType.DMA
    return pl.pallas_call(
        functools.partial(kernel, n, doc_lengths.shape[0]),
        out_shape=(
            jax.ShapeDtypeStruct(queries.shape, BF16),
            jax.ShapeDtypeStruct(keys.shape, BF16),
            jax.ShapeDtypeStruct(values.shape, BF16),
        ),
        in_specs=[pl.BlockSpec(memory_space=pltpu.SMEM)] + [any_spec] * 6,
        out_specs=(any_spec, vmem, vmem),
        scratch_shapes=[
            pltpu.VMEM((T, width), BF16),
            pltpu.VMEM((T, width), BF16),
            pltpu.VMEM((T, width), BF16),
            pltpu.VMEM((heads, T), F32),
            pltpu.VMEM((2, T, KVH * HD), BF16),
            pltpu.VMEM((T, width), BF16),
            pltpu.VMEM((KVH, 2, 5 * T, HD), BF16),
            pltpu.VMEM((4 * T, T), F32),
            pltpu.VMEM((heads, T), F32),
            pltpu.VMEM((5 * T, group * T), BF16),
            pltpu.VMEM((5 * T, group * T), BF16),
            pltpu.VMEM((HD, 5 * T), BF16),
            pltpu.VMEM((KVH, 2, T, HD), F32),
            pltpu.VMEM((2, KVH, 2, T, HD), F32),
            pltpu.VMEM((4, KVH, 2, T, HD), BF16),
            pltpu.VMEM((4, KVH, 2, T, HD), BF16),
            dma((6,)), dma((KVH,)),
            dma((4, KVH)), dma((4, KVH)), dma((4, KVH)), dma((4, KVH)),
        ],
        compiler_params=pltpu.CompilerParams(
            collective_id=0, has_side_effects=True, vmem_limit_bytes=40 * 1024 * 1024
        ),
        name="attention_grad",
    )(doc_lengths, queries, keys, values, outputs, out_grad, log_normalizer)


def solution(mesh):
    rows = P(("grp", "ctx"), None)
    in_specs = (rows,) * 5 + (P(None, ("grp", "ctx")), P("grp"))
    return jax.shard_map(
        functools.partial(body, mesh.shape["ctx"]),
        mesh=mesh, in_specs=in_specs, out_specs=(rows,) * 3, check_vma=False,
    )
```

time: 124 us -> 51.8 us (0.42)
  the two profiles are of different devices: /device:TPU:19 before, /device:TPU:0 now
where the time goes in v1:
time: 51.8 us; the launch traced here: 51.4 us
  Pallas kernels  41.6 us (80%)
  local copies, waits for them, and re-layouts  9.13 us (18%)
  between operations  0.66 us (1%)
    pallas_call x1, Pallas kernels, body(): pl.pallas_call(functools.partial(kernel, n, doc_lengths.shape[0]), out_sh...  41.6 us
    unnamed x17, local copies, waits for them, and re-layouts  9.13 us

profile of v1, /device:TPU:0, one launch (start us, length us, event | category | flops | bytes accessed | tf_op | source)
XLA Modules:
  0.0 51.4 jit_solution(8053815888576288745)
XLA Ops:
  0.6 0.0 copy-start
  0.6 1.2 %copy-done = bf16[128,4096]{1,0:T(8,128)(2,1)S(1)} copy-done((bf16[128,4096]{1,0:T(8,128)(2,1)S(1)}, bf16[128,4096]{1,0:T(8,128)(2,1)}, u32[]{:S(2)}) %copy-start) | copy-done | bytes 1048600
  1.9 0.0 copy-start.1
  1.9 1.2 %copy-done.1 = bf16[128,4096]{1,0:T(8,128)(2,1)S(1)} copy-done((bf16[128,4096]{1,0:T(8,128)(2,1)S(1)}, bf16[128,4096]{1,0:T(8,128)(2,1)}, u32[]{:S(2)}) %copy-start.1) | copy-done | bytes 1048600
  3.1 0.0 copy-start.2
  3.1 1.2 %copy-done.2 = bf16[128,4096]{1,0:T(8,128)(2,1)S(1)} copy-done((bf16[128,4096]{1,0:T(8,128)(2,1)S(1)}, bf16[128,4096]{1,0:T(8,128)(2,1)}, u32[]{:S(2)}) %copy-start.2) | copy-done | bytes 1048600
  4.3 0.0 copy-start.3
  4.3 0.9 %copy-done.3 = bf16[128,512]{1,0:T(8,128)(2,1)S(1)} copy-done((bf16[128,512]{1,0:T(8,128)(2,1)S(1)}, bf16[128,512]{1,0:T(8,128)(2,1)}, u32[]{:S(2)}) %copy-start.3) | copy-done | bytes 131096
  5.2 0.0 copy-start.4
  5.2 0.9 %copy-done.4 = bf16[128,512]{1,0:T(8,128)(2,1)S(1)} copy-done((bf16[128,512]{1,0:T(8,128)(2,1)S(1)}, bf16[128,512]{1,0:T(8,128)(2,1)}, u32[]{:S(2)}) %copy-start.4) | copy-done | bytes 131096
  6.1 0.0 copy-start.5
  6.1 0.7 %copy-done.5 = f32[32,128]{1,0:T(8,128)S(1)} copy-done((f32[32,128]{1,0:T(8,128)S(1)}, f32[32,128]{1,0:T(8,128)}, u32[]{:S(2)}) %copy-start.5) | copy-done | bytes 16408
  6.8 0.0 copy-start.6
  6.8 0.7 %copy-done.6 = s32[8]{0:T(128)S(1)} copy-done((s32[8]{0:T(128)S(1)}, s32[8]{0:T(128)}, u32[]{:S(2)}) %copy-start.6) | copy-done | bytes 56
  7.5 41.6 %attention_grad.1 = (bf16[128,4096]{1,0:T(8,128)(2,1)S(1)}, bf16[128,512]{1,0:T(8,128)(2,1)S(1)}, bf16[128,512]{1,0:T(8,128)(2,1)S(1)}) custom-call(s32[8]{0:T(128)S(1)} %copy-done.6, bf16[128,4096]{1,0:T(8,128)(2,1)S(1)} %copy-done, bf16[128,512]{1,0:T(8,128)(2,1)S(1)} %copy-done.3, bf16[128,512]{1,0:T(8,128)(2,1)S(1)} %copy-done.4, ...), custom_call_target="tpu_custom_call" | custom-call | tf_op jit(solution)/shard_map/attention_grad/pallas_call | solution.py:328
  49.1 1.0 %copy.13 = bf16[128,4096]{1,0:T(8,128)(2,1)} copy(bf16[128,4096]{1,0:T(8,128)(2,1)S(1)} %get-tuple-element.6) | data formatting | bytes 2097152
  50.1 0.7 %copy.14 = bf16[128,512]{1,0:T(8,128)(2,1)} copy(bf16[128,512]{1,0:T(8,128)(2,1)S(1)} %get-tuple-element.7) | data formatting | bytes 262144
  50.8 0.7 %copy.15 = bf16[128,512]{1,0:T(8,128)(2,1)} copy(bf16[128,512]{1,0:T(8,128)(2,1)S(1)} %get-tuple-element.8) | data formatting | bytes 262144
Async XLA Ops:
  0.6 1.2 %copy-start = (bf16[128,4096]{1,0:T(8,128)(2,1)S(1)}, bf16[128,4096]{1,0:T(8,128)(2,1)}, u32[]{:S(2)}) copy-start(bf16[128,4096]{1,0:T(8,128)(2,1)} %q_hbm.1) | copy-start | bytes 3145732
  1.9 1.2 %copy-start.1 = (bf16[128,4096]{1,0:T(8,128)(2,1)S(1)}, bf16[128,4096]{1,0:T(8,128)(2,1)}, u32[]{:S(2)}) copy-start(bf16[128,4096]{1,0:T(8,128)(2,1)} %o_hbm.1) | copy-start | bytes 3145732
  3.1 1.2 %copy-start.2 = (bf16[128,4096]{1,0:T(8,128)(2,1)S(1)}, bf16[128,4096]{1,0:T(8,128)(2,1)}, u32[]{:S(2)}) copy-start(bf16[128,4096]{1,0:T(8,128)(2,1)} %do_hbm.1) | copy-start | bytes 3145732
  4.3 0.9 %copy-start.3 = (bf16[128,512]{1,0:T(8,128)(2,1)S(1)}, bf16[128,512]{1,0:T(8,128)(2,1)}, u32[]{:S(2)}) copy-start(bf16[128,512]{1,0:T(8,128)(2,1)} %k_hbm.1) | copy-start | bytes 393220
  5.2 0.9 %copy-start.4 = (bf16[128,512]{1,0:T(8,128)(2,1)S(1)}, bf16[128,512]{1,0:T(8,128)(2,1)}, u32[]{:S(2)}) copy-start(bf16[128,512]{1,0:T(8,128)(2,1)} %v_hbm.1) | copy-start | bytes 393220
  6.1 0.7 %copy-start.5 = (f32[32,128]{1,0:T(8,128)S(1)}, f32[32,128]{1,0:T(8,128)}, u32[]{:S(2)}) copy-start(f32[32,128]{1,0:T(8,128)} %ln_hbm.1) | copy-start | bytes 49156
  6.8 0.7 %copy-start.6 = (s32[8]{0:T(128)S(1)}, s32[8]{0:T(128)}, u32[]{:S(2)}) copy-start(s32[8]{0:T(128)} %doc_ref.1) | copy-start | bytes 100

commit v2 on v1

--- a/solution.py
+++ b/solution.py
@@ -31,7 +31,7 @@
     n, docs,
     doc_ref, q_hbm, k_hbm, v_hbm, o_hbm, do_hbm, ln_hbm,
     dq_hbm, dk_ref, dv_ref,
-    q, o, do, ln, own, dq, kv, bias, rd, wbuf, gbuf, kt, acc_x, acc, bsend, brecv,
+    q, o, do, ln, own, dq, dq_sum, kv, bias, rd, wbuf, gbuf, kt, acc_x, acc, bsend, brecv,
     load_sem, store_sem, fs_sem, fr_sem, bs_sem, br_sem,
 ):
     T = q_hbm.shape[0]
@@ -150,14 +150,14 @@
         start_row = jnp.where(end <= pos_row, jnp.maximum(start_row, end), start_row)
     s_col = lax.broadcasted_iota(jnp.int32, (T, T), 0)
     t_col = lax.broadcasted_iota(jnp.int32, (T, T), 1)
-    tri1 = s_col <= t_col
-    bases = (me - 1 - 2 * c, me - 3 + 2 * c, me - 2)
+    bases = (me - 1 - 2 * c, me - 3 + 2 * c, me - 2, me - SPAN, me)
     for slot, base in enumerate(bases):
         ok = base * T + s_col >= start_row
-        b = jnp.where(ok, 0.0, -1e30).astype(F32)
-        bias[slot * T:(slot + 1) * T, :] = b
-    ok = jnp.where(tri1, me, me - SPAN) * T + s_col >= start_row
-    bias[3 * T:4 * T, :] = jnp.where(ok, 0.0, -1e30).astype(F32)
+        if slot == PB:
+            ok = ok & (s_col > t_col)
+        if slot == M:
+            ok = ok & (s_col <= t_col)
+        bias[slot * T:(slot + 1) * T, :] = jnp.where(ok, 0.0, -1e30).astype(F32)
 
     for cp in loads_rd:
         cp.wait()
@@ -175,10 +175,6 @@
     for cp in loads_q:
         cp.wait()
 
-    relay_p(0)
-    relay_x(0)
-    relay_p(1)
-
     def bwd(kind, g, target):
         return pltpu.make_async_remote_copy(
             src_ref=bsend.at[kind, g], dst_ref=brecv.at[kind, g],
@@ -229,39 +225,42 @@
     def pair_lanes(ref, h):
         return jnp.concatenate([ref[h:h + 1, :], ref[h + 1:h + 2, :]], axis=1)
 
-    def scores(g, between):
-        k_all = kv[g, 0]
-        v_all = kv[g, 1]
-        kt[...] = k_all.T
-        tri = jnp.concatenate([tri1, tri1], axis=1)
+    def tiles(g, first, last, start_sum, between=None):
+        rows = slice(first * T, (last + 1) * T)
+        k_rows = kv[g, 0, rows, :]
+        v_rows = kv[g, 1, rows, :]
+        kt[:, rows] = k_rows.T
         for p in range(group // 2):
             h = g * group + 2 * p
-            st = nt(k_all, pair_rows(q, h))
-            gp = nt(v_all, pair_rows(do, h))
+            st = nt(k_rows, pair_rows(q, h))
+            gp = nt(v_rows, pair_rows(do, h))
             shift = pair_lanes(ln, h) * LOG2E
             dot_row = pair_lanes(rd, h)
             lanes = slice(p * 2 * T, (p + 1) * 2 * T)
-            for slot in range(4):
-                rows = slice(slot * T, (slot + 1) * T)
-                s_t, g_t = st[rows], gp[rows]
-                if slot == 3:
-                    s_t = jnp.where(tri, st[M * T:], s_t)
-                    g_t = jnp.where(tri, gp[M * T:], g_t)
-                b = bias[rows, :]
+            for slot in range(first, last + 1):
+                part = slice((slot - first) * T, (slot - first + 1) * T)
+                here = slice(slot * T, (slot + 1) * T)
+                b = bias[here, :]
                 b = jnp.concatenate([b, b], axis=1)
-                w = jnp.exp2(s_t * (inv_root * LOG2E) - shift + b)
-                gs = w * (g_t - dot_row)
-                if slot == 3:
-                    wbuf[M * T:, lanes] = jnp.where(tri, w, 0.0).astype(BF16)
-                    gbuf[M * T:, lanes] = jnp.where(tri, gs, 0.0).astype(BF16)
-                    w = jnp.where(tri, 0.0, w)
-                    gs = jnp.where(tri, 0.0, gs)
-                wbuf[rows, lanes] = w.astype(BF16)
-                gbuf[rows, lanes] = gs.astype(BF16)
-            dqt = nn(kt[...], gbuf[:, lanes]) * inv_root
-            dq[:, h * HD:(h + 1) * HD] = dqt[:, :T].T.astype(BF16)
-            dq[:, (h + 1) * HD:(h + 2) * HD] = dqt[:, T:].T.astype(BF16)
-            between(p)
+                w = jnp.exp2(st[part] * (inv_root * LOG2E) - shift + b)
+                gs = w * (gp[part] - dot_row)
+                wbuf[here, lanes] = w.astype(BF16)
+                gbuf[here, lanes] = gs.astype(BF16)
+            dqt = nn(kt[:, rows], gbuf[rows, lanes])
+            sums = slice(h * T, (h + 2) * T)
+            if start_sum:
+                dq_sum[:, sums] = dqt
+            elif last != PB:
+                dq_sum[:, sums] += dqt
+            else:
+                dqt = (dq_sum[:, sums] + dqt) * inv_root
+                dq[:, h * HD:(h + 1) * HD] = dqt[:, :T].T.astype(BF16)
+                dq[:, (h + 1) * HD:(h + 2) * HD] = dqt[:, T:].T.astype(BF16)
+            if between is not None:
+                between(p)
+        dk = nn(gbuf[rows, :], stacked(q, g)) * inv_root
+        dv = nn(wbuf[rows, :], stacked(do, g))
+        return dk, dv
 
     def stacked(ref, g):
         return jnp.concatenate(
@@ -269,35 +268,38 @@
         )
 
     for g in range(KVH):
-        if g > 0:
-            relay_x(g)
-            if g + 1 < KVH:
-                relay_p(g + 1)
+        for a, part in enumerate(tiles(g, M, M, True)):
+            acc[0, g, a] = part
+        relay_p(g)
+
+    relay_x(0)
+    relay_x(1)
+    for g in range(KVH):
         arrived(g)
 
         def between(p, g=g):
-            if p == 1 and g >= 1:
+            if p == 0 and g + 2 < KVH:
+                relay_x(g + 2)
+            if p == 3 and g >= 1:
                 hop2(g - 1)
-            if p == 3 and g >= 1:
-                hop3(g - 1)
-
-        scores(g, between)
-        store(g).start()
-        dk = nn(gbuf[...], stacked(q, g)) * inv_root
-        dv = nn(wbuf[...], stacked(do, g))
+
+        dk, dv = tiles(g, CX, X, False, between)
         for kind in (CX, C):
             bsend[kind, g, 0] = dk[kind * T:(kind + 1) * T].astype(BF16)
             bsend[kind, g, 1] = dv[kind * T:(kind + 1) * T].astype(BF16)
             bwd(kind, g, mate).start()
-        for a, part in enumerate((dk, dv)):
-            acc_x[g, a] = part[X * T:(X + 1) * T]
-            acc[1, g, a] = part[PB * T:(PB + 1) * T]
-            acc[0, g, a] = part[M * T:]
-    hop2(KVH - 1)
-    for g in range(KVH - 1):
+        acc_x[g, 0] = dk[X * T:]
+        acc_x[g, 1] = dv[X * T:]
+
+    for g in range(KVH):
+        for a, part in enumerate(tiles(g, PB, PB, False)):
+            acc[1, g, a] = part
+        store(g).start()
+        if g == 0:
+            hop2(KVH - 1)
+        hop3(g)
+    for g in range(KVH):
         hop4(g)
-    hop3(KVH - 1)
-    hop4(KVH - 1)
 
     for g in range(KVH):
         store(g).wait()
@@ -341,8 +343,9 @@
             pltpu.VMEM((heads, T), F32),
             pltpu.VMEM((2, T, KVH * HD), BF16),
             pltpu.VMEM((T, width), BF16),
+            pltpu.VMEM((HD, heads * T), F32),
             pltpu.VMEM((KVH, 2, 5 * T, HD), BF16),
-            pltpu.VMEM((4 * T, T), F32),
+            pltpu.VMEM((5 * T, T), F32),
             pltpu.VMEM((heads, T), F32),
             pltpu.VMEM((5 * T, group * T), BF16),
             pltpu.VMEM((5 * T, group * T), BF16),
@@ -355,7 +358,7 @@
             dma((4, KVH)), dma((4, KVH)), dma((4, KVH)), dma((4, KVH)),
         ],
         compiler_params=pltpu.CompilerParams(
-            collective_id=0, has_side_effects=True, vmem_limit_bytes=40 * 1024 * 1024
+            collective_id=0, has_side_effects=True, vmem_limit_bytes=60 * 1024 * 1024
         ),
         name="attention_grad",
     )(doc_lengths, queries, keys, values, outputs, out_grad, log_normalizer)

time: 51.8 us -> 35.9 us (0.69)
  Pallas kernels: 41.6 us -> 31.1 us
  local copies, waits for them, and re-layouts: 9.13 us -> 3.93 us
    pallas_call x1, Pallas kernels: 41.6 us -> 31.1 us  [body(): pl.pallas_call(functools.partial(kernel, n, doc_lengths.shape[0]), out_sh...]
    unnamed x17 -> x7, local copies, waits for them, and re-layouts: 9.13 us -> 3.93 us
where the time goes in v2:
time: 35.9 us; the launch traced here: 35.7 us
  Pallas kernels  31.1 us (87%)
  local copies, waits for them, and re-layouts  3.93 us (11%)
  between operations  0.65 us (2%)
    pallas_call x1, Pallas kernels, body(): pl.pallas_call(functools.partial(kernel, n, doc_lengths.shape[0]), out_sh...  31.1 us
    unnamed x7, local copies, waits for them, and re-layouts  3.93 us

profile of v2, /device:TPU:0, one launch (start us, length us, event | category | flops | bytes accessed | tf_op | source)
XLA Modules:
  0.0 35.7 jit_solution(7938885483483730887)
XLA Ops:
  0.6 31.1 %attention_grad.1 = (bf16[128,4096]{1,0:T(8,128)(2,1)}, bf16[128,512]{1,0:T(8,128)(2,1)}, bf16[128,512]{1,0:T(8,128)(2,1)}) custom-call(s32[8]{0:T(128)} %doc_ref.1, bf16[128,4096]{1,0:T(8,128)(2,1)} %q_hbm.1, bf16[128,512]{1,0:T(8,128)(2,1)} %k_hbm.1, bf16[128,512]{1,0:T(8,128)(2,1)} %v_hbm.1, bf16[128,4096]{1,0:T(8,128)(2,1)} %o_hbm.1, ...), custom_call_target="tpu_custom_call" | custom-call | tf_op jit(solution)/shard_map/attention_grad/pallas_call | solution.py:330
  31.8 0.0 copy-start.1
  31.8 2.3 %copy.13 = bf16[128,4096]{1,0:T(8,128)(2,1)} copy(bf16[128,4096]{1,0:T(8,128)(2,1)} %get-tuple-element.6) | data formatting | bytes 2097152
  34.1 0.0 copy-done.1
  34.1 0.0 copy-start
  34.1 0.7 %copy.14 = bf16[128,512]{1,0:T(8,128)(2,1)} copy(bf16[128,512]{1,0:T(8,128)(2,1)S(1)} %copy-done.1) | data formatting | bytes 262144
  34.7 0.3 copy-done
  35.0 0.7 %copy.15 = bf16[128,512]{1,0:T(8,128)(2,1)} copy(bf16[128,512]{1,0:T(8,128)(2,1)S(1)} %copy-done) | data formatting | bytes 262144
Async XLA Ops:
  31.8 2.3 %copy-start.1 = (bf16[128,512]{1,0:T(8,128)(2,1)S(1)}, bf16[128,512]{1,0:T(8,128)(2,1)}, u32[]{:S(2)}) copy-start(bf16[128,512]{1,0:T(8,128)(2,1)} %get-tuple-element.7) | copy-start | bytes 393220
  34.1 1.0 %copy-start = (bf16[128,512]{1,0:T(8,128)(2,1)S(1)}, bf16[128,512]{1,0:T(8,128)(2,1)}, u32[]{:S(2)}) copy-start(bf16[128,512]{1,0:T(8,128)(2,1)} %get-tuple-element.8) | copy-start | bytes 393220

commit v3 on v2

--- a/solution.py
+++ b/solution.py
@@ -11,6 +11,7 @@
 HD = 128
 KVH = 4
 SPAN = 4
+EARLY = 2
 LOG2E = 1.0 / math.log(2.0)
 MESH = pl.DeviceIdType.MESH
 F32 = jnp.float32
@@ -30,8 +31,8 @@
 def kernel(
     n, docs,
     doc_ref, q_hbm, k_hbm, v_hbm, o_hbm, do_hbm, ln_hbm,
-    dq_hbm, dk_ref, dv_ref,
-    q, o, do, ln, own, dq, dq_sum, kv, bias, rd, wbuf, gbuf, kt, acc_x, acc, bsend, brecv,
+    dq_hbm, dk_hbm, dv_hbm,
+    q, o, do, ln, own, dq, dq_sum, dk_ref, dv_ref, kv, bias, rd, wbuf, gbuf, kt, acc_x, acc, bsend, brecv,
     load_sem, store_sem, fs_sem, fr_sem, bs_sem, br_sem,
 ):
     T = q_hbm.shape[0]
@@ -225,6 +226,8 @@
     def pair_lanes(ref, h):
         return jnp.concatenate([ref[h:h + 1, :], ref[h + 1:h + 2, :]], axis=1)
 
+    tri = jnp.concatenate([s_col <= t_col] * 2, axis=1)
+
     def tiles(g, first, last, start_sum, between=None):
         rows = slice(first * T, (last + 1) * T)
         k_rows = kv[g, 0, rows, :]
@@ -237,7 +240,22 @@
             shift = pair_lanes(ln, h) * LOG2E
             dot_row = pair_lanes(rd, h)
             lanes = slice(p * 2 * T, (p + 1) * 2 * T)
-            for slot in range(first, last + 1):
+            if first == PB and last == M:
+                old, own_rows = slice(PB * T, M * T), slice(M * T, (M + 1) * T)
+                b = jnp.maximum(bias[old, :], bias[own_rows, :])
+                b = jnp.concatenate([b, b], axis=1)
+                s_t = jnp.where(tri, st[T:], st[:T])
+                g_t = jnp.where(tri, gp[T:], gp[:T])
+                w = jnp.exp2(s_t * (inv_root * LOG2E) - shift + b)
+                gs = w * (g_t - dot_row)
+                wbuf[old, lanes] = jnp.where(tri, 0.0, w).astype(BF16)
+                gbuf[old, lanes] = jnp.where(tri, 0.0, gs).astype(BF16)
+                wbuf[own_rows, lanes] = jnp.where(tri, w, 0.0).astype(BF16)
+                gbuf[own_rows, lanes] = jnp.where(tri, gs, 0.0).astype(BF16)
+                slots = ()
+            else:
+                slots = range(first, last + 1)
+            for slot in slots:
                 part = slice((slot - first) * T, (slot - first + 1) * T)
                 here = slice(slot * T, (slot + 1) * T)
                 b = bias[here, :]
@@ -250,7 +268,7 @@
             sums = slice(h * T, (h + 2) * T)
             if start_sum:
                 dq_sum[:, sums] = dqt
-            elif last != PB:
+            elif last == X:
                 dq_sum[:, sums] += dqt
             else:
                 dqt = (dq_sum[:, sums] + dqt) * inv_root
@@ -268,8 +286,9 @@
         )
 
     for g in range(KVH):
-        for a, part in enumerate(tiles(g, M, M, True)):
-            acc[0, g, a] = part
+        if g < EARLY:
+            for a, part in enumerate(tiles(g, M, M, True)):
+                acc[0, g, a] = part
         relay_p(g)
 
     relay_x(0)
@@ -283,7 +302,7 @@
             if p == 3 and g >= 1:
                 hop2(g - 1)
 
-        dk, dv = tiles(g, CX, X, False, between)
+        dk, dv = tiles(g, CX, X, g >= EARLY, between)
         for kind in (CX, C):
             bsend[kind, g, 0] = dk[kind * T:(kind + 1) * T].astype(BF16)
             bsend[kind, g, 1] = dv[kind * T:(kind + 1) * T].astype(BF16)
@@ -292,15 +311,25 @@
         acc_x[g, 1] = dv[X * T:]
 
     for g in range(KVH):
-        for a, part in enumerate(tiles(g, PB, PB, False)):
-            acc[1, g, a] = part
+        for a, part in enumerate(tiles(g, PB, PB if g < EARLY else M, False)):
+            acc[1, g, a] = part[:T]
+            if g >= EARLY:
+                acc[0, g, a] = part[T:]
         store(g).start()
         if g == 0:
             hop2(KVH - 1)
         hop3(g)
     for g in range(KVH):
         hop4(g)
-
+    last = [
+        pltpu.make_async_copy(dk_ref, dk_hbm, store_sem.at[KVH]),
+        pltpu.make_async_copy(dv_ref, dv_hbm, store_sem.at[KVH + 1]),
+    ]
+    for cp in last:
+        cp.start()
+
+    for cp in last:
+        cp.wait()
     for g in range(KVH):
         store(g).wait()
         for kind, target in ((CX, mate), (C, mate), (X, peer)):
@@ -325,7 +354,6 @@
     heads = width // HD
     group = heads // KVH
     any_spec = pl.BlockSpec(memory_space=pl.ANY)
-    vmem = pl.BlockSpec(memory_space=pltpu.VMEM)
     dma = pltpu.SemaphoreType.DMA
     return pl.pallas_call(
         functools.partial(kernel, n, doc_lengths.shape[0]),
@@ -335,7 +363,7 @@
             jax.ShapeDtypeStruct(values.shape, BF16),
         ),
         in_specs=[pl.BlockSpec(memory_space=pltpu.SMEM)] + [any_spec] * 6,
-        out_specs=(any_spec, vmem, vmem),
+        out_specs=(any_spec,) * 3,
         scratch_shapes=[
             pltpu.VMEM((T, width), BF16),
             pltpu.VMEM((T, width), BF16),
@@ -344,6 +372,8 @@
             pltpu.VMEM((2, T, KVH * HD), BF16),
             pltpu.VMEM((T, width), BF16),
             pltpu.VMEM((HD, heads * T), F32),
+            pltpu.VMEM((T, KVH * HD), BF16),
+            pltpu.VMEM((T, KVH * HD), BF16),
             pltpu.VMEM((KVH, 2, 5 * T, HD), BF16),
             pltpu.VMEM((5 * T, T), F32),
             pltpu.VMEM((heads, T), F32),
@@ -354,7 +384,7 @@
             pltpu.VMEM((2, KVH, 2, T, HD), F32),
             pltpu.VMEM((4, KVH, 2, T, HD), BF16),
             pltpu.VMEM((4, KVH, 2, T, HD), BF16),
-            dma((6,)), dma((KVH,)),
+            dma((6,)), dma((KVH + 2,)),
             dma((4, KVH)), dma((4, KVH)), dma((4, KVH)), dma((4, KVH)),
         ],
         compiler_params=pltpu.CompilerParams(

time: 35.9 us -> 35.9 us (level)
  no operation moved by 1% of the time
where the time goes in v3:
time: 35.9 us; the launch traced here: 35.7 us
  Pallas kernels  31.1 us (87%)
  local copies, waits for them, and re-layouts  3.93 us (11%)
  between operations  0.65 us (2%)
    pallas_call x1, Pallas kernels, body(): pl.pallas_call(functools.partial(kernel, n, doc_lengths.shape[0]), out_sh...  31.1 us
    unnamed x7, local copies, waits for them, and re-layouts  3.93 us

profile of v3, /device:TPU:0, one launch (start us, length us, event | category | flops | bytes accessed | tf_op | source)
XLA Modules:
  0.0 35.7 jit_solution(7899266387677030152)
XLA Ops:
  0.6 31.1 %attention_grad.1 = (bf16[128,4096]{1,0:T(8,128)(2,1)}, bf16[128,512]{1,0:T(8,128)(2,1)}, bf16[128,512]{1,0:T(8,128)(2,1)}) custom-call(s32[8]{0:T(128)} %doc_ref.1, bf16[128,4096]{1,0:T(8,128)(2,1)} %q_hbm.1, bf16[128,512]{1,0:T(8,128)(2,1)} %k_hbm.1, bf16[128,512]{1,0:T(8,128)(2,1)} %v_hbm.1, bf16[128,4096]{1,0:T(8,128)(2,1)} %o_hbm.1, ...), custom_call_target="tpu_custom_call" | custom-call | tf_op jit(solution)/shard_map/attention_grad/pallas_call | solution.py:358
  31.7 0.0 copy-start.1
  31.8 2.3 %copy.13 = bf16[128,4096]{1,0:T(8,128)(2,1)} copy(bf16[128,4096]{1,0:T(8,128)(2,1)} %get-tuple-element.6) | data formatting | bytes 2097152
  34.1 0.0 copy-done.1
  34.1 0.0 copy-start
  34.1 0.7 %copy.14 = bf16[128,512]{1,0:T(8,128)(2,1)} copy(bf16[128,512]{1,0:T(8,128)(2,1)S(1)} %copy-done.1) | data formatting | bytes 262144
  34.7 0.3 copy-done
  35.0 0.7 %copy.15 = bf16[128,512]{1,0:T(8,128)(2,1)} copy(bf16[128,512]{1,0:T(8,128)(2,1)S(1)} %copy-done) | data formatting | bytes 262144
Async XLA Ops:
  31.7 2.3 %copy-start.1 = (bf16[128,512]{1,0:T(8,128)(2,1)S(1)}, bf16[128,512]{1,0:T(8,128)(2,1)}, u32[]{:S(2)}) copy-start(bf16[128,512]{1,0:T(8,128)(2,1)} %get-tuple-element.7) | copy-start | bytes 393220
  34.1 1.0 %copy-start = (bf16[128,512]{1,0:T(8,128)(2,1)S(1)}, bf16[128,512]{1,0:T(8,128)(2,1)}, u32[]{:S(2)}) copy-start(bf16[128,512]{1,0:T(8,128)(2,1)} %get-tuple-element.8) | copy-start | bytes 393220

commit v4 on v3

--- a/solution.py
+++ b/solution.py
@@ -299,7 +299,7 @@
         def between(p, g=g):
             if p == 0 and g + 2 < KVH:
                 relay_x(g + 2)
-            if p == 3 and g >= 1:
+            if p == 1 and g >= 1:
                 hop2(g - 1)
 
         dk, dv = tiles(g, CX, X, g >= EARLY, between)

time: 35.9 us -> 36.8 us (1.025)
  Pallas kernels: 31.1 us -> 32 us
    pallas_call x1, Pallas kernels: 31.1 us -> 32 us  [body(): pl.pallas_call(functools.partial(kernel, n, doc_lengths.shape[0]), out_sh...]
where the time goes in v4:
time: 36.8 us; the launch traced here: 36.6 us
  Pallas kernels  32 us (87%)
  local copies, waits for them, and re-layouts  3.93 us (11%)
  between operations  0.65 us (2%)
    pallas_call x1, Pallas kernels, body(): pl.pallas_call(functools.partial(kernel, n, doc_lengths.shape[0]), out_sh...  32 us
    unnamed x7, local copies, waits for them, and re-layouts  3.93 us

profile of v4, /device:TPU:0, one launch (start us, length us, event | category | flops | bytes accessed | tf_op | source)
XLA Modules:
  0.0 36.6 jit_solution(14124760775850957462)
XLA Ops:
  0.6 32.0 %attention_grad.1 = (bf16[128,4096]{1,0:T(8,128)(2,1)}, bf16[128,512]{1,0:T(8,128)(2,1)}, bf16[128,512]{1,0:T(8,128)(2,1)}) custom-call(s32[8]{0:T(128)} %doc_ref.1, bf16[128,4096]{1,0:T(8,128)(2,1)} %q_hbm.1, bf16[128,512]{1,0:T(8,128)(2,1)} %k_hbm.1, bf16[128,512]{1,0:T(8,128)(2,1)} %v_hbm.1, bf16[128,4096]{1,0:T(8,128)(2,1)} %o_hbm.1, ...), custom_call_target="tpu_custom_call" | custom-call | tf_op jit(solution)/shard_map/attention_grad/pallas_call | solution.py:358
  32.6 0.0 copy-start.1
  32.7 2.3 %copy.13 = bf16[128,4096]{1,0:T(8,128)(2,1)} copy(bf16[128,4096]{1,0:T(8,128)(2,1)} %get-tuple-element.6) | data formatting | bytes 2097152
  35.0 0.0 copy-done.1
  35.0 0.0 copy-start
  35.0 0.7 %copy.14 = bf16[128,512]{1,0:T(8,128)(2,1)} copy(bf16[128,512]{1,0:T(8,128)(2,1)S(1)} %copy-done.1) | data formatting | bytes 262144
  35.6 0.3 copy-done
  35.9 0.7 %copy.15 = bf16[128,512]{1,0:T(8,128)(2,1)} copy(bf16[128,512]{1,0:T(8,128)(2,1)S(1)} %copy-done) | data formatting | bytes 262144
Async XLA Ops:
  32.6 2.3 %copy-start.1 = (bf16[128,512]{1,0:T(8,128)(2,1)S(1)}, bf16[128,512]{1,0:T(8,128)(2,1)}, u32[]{:S(2)}) copy-start(bf16[128,512]{1,0:T(8,128)(2,1)} %get-tuple-element.7) | copy-start | bytes 393220
  35.0 1.0 %copy-start = (bf16[128,512]{1,0:T(8,128)(2,1)S(1)}, bf16[128,512]{1,0:T(8,128)(2,1)}, u32[]{:S(2)}) copy-start(bf16[128,512]{1,0:T(8,128)(2,1)} %get-tuple-element.8) | copy-start | bytes 393220
